TPU v7x, 128 devices: a whole 4x4x4 slice. The times are simulated.
128 devices in a mesh: section: 4 (over z), dev: 32 (over y, x, core).
Axes of the slice: x: 4, y: 4, z: 4, core: 2. Of those that a mesh axis runs over, the one named last changes fastest.
Arguments:
- points: float32 [3, 3, 524288], P(None, None, ('section', 'dev')), may hold values from -1 to 1
- weights: float32 [3, 524288], P(None, ('section', 'dev')), may hold values from 0.2 to 0.5
- density: float32 [2, 524288], P(None, ('section', 'dev')), may hold values from -6 to 6
- near_pairs: int32 [3, 16384], P(None, ('section', 'dev')), may hold values from 0 to 4095, as said below
- gap_pairs: int32 [3, 4096], P(None, ('section', 'dev')), may hold values from 0 to 4095, as said below
Outputs:
- potentials: float32 [2, 524288], P(None, ('section', 'dev'))
Inputs may be any that keep to these rules, and one draw needn't show every extreme that they name: `near_pairs`: column t belongs to device t // 128 of section+dev. Row 0 names a cluster held by that device, row 1 a cluster held by a device of the same section whose dev index differs from the owner's by at most 2, row 2 is 0 or 1. The first 32 columns of each device are the self pairs of its clusters in order and are always listed; column 32 of each device is listed and names a cluster exactly 2 dev indices away; some device lists all its columns. `gap_pairs`: column t belongs to device t // 32 of section+dev. Row 0 names a cluster held by that device, row 1 a cluster of another section held by the device of the same index along dev, row 2 is 0 or 1; some device lists all its columns.
All inputs are finite; a program needn't handle non-finite values.
Results may differ from a plain program's by a relative error of at most 0.0001.
Values sent between devices are 32-bit elements; how exact they have to be, the bound alone decides.
No kernel may reach another device: no remote copies, remote signals or barrier semaphores. Data moves between devices by JAX's collectives and lax.ppermute only.
A program may use at most 64 MiB of HBM per device.

v0:
```python
import math

import jax
import jax.numpy as jnp
from jax import lax
from jax.sharding import PartitionSpec as P

PANEL_CL = 128


smoothing = 0.02
green_scale = 0.25 / math.pi


def passed_along(block, axis, distance):
    devices = range(lax.axis_size(axis))
    route = [(i - distance, i) for i in devices if i - distance in devices]
    return lax.ppermute(block, axis, route)


def pair_terms(block_a, block_b, listed, twice):
    groups, rows_count, width = block_a.shape
    quad_count = (rows_count - 2) // 4
    pos_a = block_a[:, : 3 * quad_count].reshape(groups, 3, quad_count, width)
    pos_b = block_b[:, : 3 * quad_count].reshape(groups, 3, quad_count, width)
    w_a = block_a[:, 3 * quad_count : 4 * quad_count]
    w_b = block_b[:, 3 * quad_count : 4 * quad_count]
    dens_a = block_a[:, 4 * quad_count :]
    dens_b = block_b[:, 4 * quad_count :]
    term_a = jnp.zeros((groups, 2, width), jnp.float32)
    term_b = jnp.zeros((groups, 2, width), jnp.float32)
    for point_a in range(quad_count):
        load_a = w_a[:, point_a, None, :] * dens_a
        for point_b in range(quad_count):
            load_b = w_b[:, point_b, None, :] * dens_b
            step_x = pos_a[:, 0, point_a, :, None] - pos_b[:, 0, point_b, None, :]
            step_y = pos_a[:, 1, point_a, :, None] - pos_b[:, 1, point_b, None, :]
            step_z = pos_a[:, 2, point_a, :, None] - pos_b[:, 2, point_b, None, :]
            distance = step_x * step_x + step_y * step_y + step_z * step_z + smoothing * smoothing
            kernel_tile = green_scale / jnp.sqrt(distance)
            term_a = term_a + w_a[:, point_a, None, :] * jnp.einsum(
                "gab,grb->gra", kernel_tile, load_b, precision=lax.Precision.HIGHEST
            )
            term_b = term_b + w_b[:, point_b, None, :] * jnp.einsum(
                "gab,gra->grb", kernel_tile, load_a, precision=lax.Precision.HIGHEST
            )
    term_a = term_a * listed[:, None, None]
    term_b = term_b * (listed * twice)[:, None, None]
    return (term_a, term_b)


def accumulate(panel_table, first_pos, second_pos, listed, twice, table_clusters):
    rows_count = panel_table.shape[0]
    blocks = panel_table.reshape(rows_count, table_clusters, PANEL_CL)
    slot_count = first_pos.shape[0]
    group_size = math.gcd(slot_count, 32)
    group_count = slot_count // group_size

    def one_group(items):
        first_set, second_set, live_set, twice_set = items
        block_a = jnp.transpose(blocks[:, first_set], (1, 0, 2))
        block_b = jnp.transpose(blocks[:, second_set], (1, 0, 2))
        return pair_terms(block_a, block_b, live_set, twice_set)

    items = (
        first_pos.reshape(group_count, group_size),
        second_pos.reshape(group_count, group_size),
        listed.reshape(group_count, group_size),
        twice.reshape(group_count, group_size),
    )
    terms_a, terms_b = lax.map(one_group, items)
    terms_a = jnp.transpose(terms_a.reshape(slot_count, 2, PANEL_CL), (1, 0, 2))
    terms_b = jnp.transpose(terms_b.reshape(slot_count, 2, PANEL_CL), (1, 0, 2))
    totals = jnp.zeros((2, table_clusters, PANEL_CL), jnp.float32)
    totals = totals.at[:, first_pos].add(terms_a)
    totals = totals.at[:, second_pos].add(terms_b)
    return totals.reshape(2, table_clusters * PANEL_CL)


def facing_part(local_table, gap_pairs, local_clusters, section_clusters):
    gap_first = gap_pairs[0]
    gap_second = gap_pairs[1]
    gap_listed = gap_pairs[2].astype(jnp.float32)
    gap_twice = (gap_first != gap_second).astype(jnp.float32)
    facing_table = lax.all_gather(local_table, "section", axis=1, tiled=True)
    facing_clusters = facing_table.shape[1] // PANEL_CL
    section_place = lax.axis_index("section")
    gap_a = section_place * local_clusters + gap_first % local_clusters
    gap_b = gap_second // section_clusters * local_clusters + gap_second % local_clusters
    gap_totals = accumulate(facing_table, gap_a, gap_b, gap_listed, gap_twice, facing_clusters)
    return lax.psum_scatter(gap_totals, "section", scatter_dimension=1, tiled=True)


def per_device(points, weights, density, near_pairs, gap_pairs):
    quad_count = points.shape[1]
    local_panels = points.shape[2]
    local_clusters = local_panels // PANEL_CL
    section_clusters = local_clusters * lax.axis_size("dev")
    local_table = jnp.concatenate(
        [points.reshape(3 * quad_count, local_panels), weights, density], 0
    )
    near_first = near_pairs[0]
    near_second = near_pairs[1]
    near_listed = near_pairs[2].astype(jnp.float32)
    near_twice = (near_first != near_second).astype(jnp.float32)
    section_place = lax.axis_index("section")
    dev_place = lax.axis_index("dev")
    pieces = [local_table, local_table, local_table, local_table, local_table]
    for place in range(5):
        if place != 2:
            pieces[place] = passed_along(local_table, "dev", 2 - place)
    nearby_table = jnp.concatenate(pieces, 1)
    base = section_place * section_clusters + (dev_place - 2) * local_clusters
    near_totals = accumulate(
        nearby_table,
        near_first - base,
        near_second - base,
        near_listed,
        near_twice,
        5 * local_clusters,
    )
    near_totals = near_totals.reshape(2, 5, local_panels)
    summed = near_totals[:, 2]
    for place in range(5):
        if place != 2:
            summed = summed + passed_along(near_totals[:, place], "dev", place - 2)
    summed = summed + facing_part(local_table, gap_pairs, local_clusters, section_clusters)
    return summed


def solution(mesh):
    placed = (
        P(None, None, ("section", "dev")),
        P(None, ("section", "dev")),
        P(None, ("section", "dev")),
        P(None, ("section", "dev")),
        P(None, ("section", "dev")),
    )
    return jax.shard_map(
        per_device,
        mesh=mesh,
        in_specs=placed,
        out_specs=P(None, ("section", "dev")),
        check_vma=False,
    )
```

profile of v0, /device:TPU:41, one launch (start us, length us, event | category | flops | bytes accessed | tf_op | source)
XLA Modules:
  0.0 502.8 jit_solution(1264819455733787381)
XLA Ops:
  11.6 4.0 collective-permute-start.1
  17.5 4.3 collective-permute-start.3
  21.8 12.2 %all_gather.3 = f32[14,16384]{1,0:T(8,128)S(1)} all-gather(f32[14,4096]{1,0:T(8,128)S(1)} %pad_maximum_fusion), channel_id=1, replica_groups=mesh['section'=4,'dev'=32] {'section'}, dimensions={1}, use_global_device_ids=true | all-gather | bytes 1146880 | tf_op jit(solution)/shard_map/all_gather | solution.py:85
  36.3 5.1 %fusion.244 = f32[32,2,128]{2,1,0:T(2,128)S(1)} fusion(f32[32,128]{1,0:T(8,128)S(1)} %get-tuple-element.163, f32[32,128]{1,0:T(8,128)S(1)} %get-tuple-element.154, f32[32,128]{1,0:T(8,128)S(1)} %get-tuple-element.164, f32[32,128]{1,0:T(8,128)S(1)} %get-tuple-element.155, f32[32,128]{1,0:T(8,128)S(1)} %get-tuple-element.165, ...), kind=kOutput, calls=%fused_computation.302 | convolution fusion | flops 17833984 | bytes 180224 | tf_op jit(solution)/shard_map/while/body/eval_jaxpr/gab,grb->gra/dot_general | solution.py:41
  52.7 3.8 fusion.286
  67.8 3.8 fusion.270
  71.6 5.1 %fusion.291 = f32[32,2,128]{2,1,0:T(2,128)S(1)} fusion(f32[32,2,128]{2,1,0:T(2,128)S(1)} %fusion.244, f32[32,128]{1,0:T(8,128)S(1)} %get-tuple-element.160, f32[32,128]{1,0:T(8,128)S(1)} %get-tuple-element.161, f32[32,128]{1,0:T(8,128)S(1)} %get-tuple-element.162, f32[32,128]{1,0:T(8,128)S(1)} %get-tuple-element.154, ...), kind=kOutput, calls=%fused_computation.349 | convolution fusion | flops 17842176 | bytes 212992 | tf_op jit(solution)/shard_map/while/body/eval_jaxpr/gab,grb->gra/dot_general | solution.py:41
  76.7 5.1 %fusion.288 = f32[32,2,128]{2,1,0:T(2,128)S(1)} fusion(f32[32,2,128]{2,1,0:T(2,128)S(1)} %fusion.291, f32[32,128]{1,0:T(8,128)S(1)} %get-tuple-element.158, f32[32,128]{1,0:T(8,128)S(1)} %get-tuple-element.159, f32[32,128]{1,0:T(8,128)S(1)} %get-tuple-element.157, f32[32,128]{1,0:T(8,128)S(1)} %get-tuple-element.154, ...), kind=kOutput, calls=%fused_computation.346 | convolution fusion | flops 17850368 | bytes 229376 | tf_op jit(solution)/shard_map/while/body/eval_jaxpr/gab,grb->gra/dot_general | solution.py:41
  81.8 5.1 %fusion.284 = f32[32,2,128]{2,1,0:T(2,128)S(1)} fusion(f32[32,2,128]{2,1,0:T(2,128)S(1)} %fusion.288, f32[32,128]{1,0:T(8,128)S(1)} %get-tuple-element.151, f32[32,128]{1,0:T(8,128)S(1)} %get-tuple-element.152, f32[32,128]{1,0:T(8,128)S(1)} %get-tuple-element.153, f32[32,128]{1,0:T(8,128)S(1)} %get-tuple-element.163, ...), kind=kOutput, calls=%fused_computation.342 | convolution fusion | flops 17850368 | bytes 229376 | tf_op jit(solution)/shard_map/while/body/eval_jaxpr/gab,grb->gra/dot_general | solution.py:41
  86.9 5.1 %fusion.280 = f32[32,2,128]{2,1,0:T(2,128)S(1)} fusion(f32[32,2,128]{2,1,0:T(2,128)S(1)} %fusion.284, f32[32,128]{1,0:T(8,128)S(1)} %get-tuple-element.151, f32[32,128]{1,0:T(8,128)S(1)} %get-tuple-element.152, f32[32,128]{1,0:T(8,128)S(1)} %get-tuple-element.153, f32[32,128]{1,0:T(8,128)S(1)} %get-tuple-element.160, ...), kind=kOutput, calls=%fused_computation.338 | convolution fusion | flops 17850368 | bytes 229376 | tf_op jit(solution)/shard_map/while/body/eval_jaxpr/gab,grb->gra/dot_general | solution.py:41
  92.1 5.1 %fusion.276 = f32[32,2,128]{2,1,0:T(2,128)S(1)} fusion(f32[32,2,128]{2,1,0:T(2,128)S(1)} %fusion.280, f32[32,128]{1,0:T(8,128)S(1)} %get-tuple-element.151, f32[32,128]{1,0:T(8,128)S(1)} %get-tuple-element.152, f32[32,128]{1,0:T(8,128)S(1)} %get-tuple-element.153, f32[32,128]{1,0:T(8,128)S(1)} %get-tuple-element.158, ...), kind=kOutput, calls=%fused_computation.334 | convolution fusion | flops 17850368 | bytes 229376 | tf_op jit(solution)/shard_map/while/body/eval_jaxpr/gab,grb->gra/dot_general | solution.py:41
  97.2 5.4 %fusion.272 = f32[32,2,128]{2,1,0:T(2,128)S(1)} fusion(f32[32,2,128]{2,1,0:T(2,128)S(1)} %fusion.276, f32[32,128]{1,0:T(8,128)S(1)} %get-tuple-element.149, f32[32,128]{1,0:T(8,128)S(1)} %get-tuple-element.150, f32[32,128]{1,0:T(8,128)S(1)} %get-tuple-element.148, f32[32,128]{1,0:T(8,128)S(1)} %get-tuple-element.163, ...), kind=kOutput, calls=%fused_computation.330 | convolution fusion | flops 17850368 | bytes 229376 | tf_op jit(solution)/shard_map/while/body/eval_jaxpr/gab,grb->gra/dot_general | solution.py:41
  102.5 5.1 %fusion.268 = f32[32,2,128]{2,1,0:T(2,128)S(1)} fusion(f32[32,2,128]{2,1,0:T(2,128)S(1)} %fusion.272, f32[32,128]{1,0:T(8,128)S(1)} %get-tuple-element.149, f32[32,128]{1,0:T(8,128)S(1)} %get-tuple-element.150, f32[32,128]{1,0:T(8,128)S(1)} %get-tuple-element.148, f32[32,128]{1,0:T(8,128)S(1)} %get-tuple-element.160, ...), kind=kOutput, calls=%fused_computation.326 | convolution fusion | flops 17850368 | bytes 229376 | tf_op jit(solution)/shard_map/while/body/eval_jaxpr/gab,grb->gra/dot_general | solution.py:41
  107.7 3.8 fusion.266
  111.4 5.1 %fusion.263 = f32[32,2,128]{2,1,0:T(2,128)S(1)} fusion(f32[32,2,128]{2,1,0:T(2,128)S(1)} %fusion.268, f32[32,128]{1,0:T(8,128)S(1)} %get-tuple-element.149, f32[32,128]{1,0:T(8,128)S(1)} %get-tuple-element.150, f32[32,128]{1,0:T(8,128)S(1)} %get-tuple-element.148, f32[32,128]{1,0:T(8,128)S(1)} %get-tuple-element.158, ...), kind=kOutput, calls=%fused_computation.321 | convolution fusion | flops 17858560 | bytes 229888 | tf_op jit(solution)/shard_map/while/body/eval_jaxpr/gab,grb->gra/dot_general | solution.py:41
  119.9 5.0 copy.24
  127.7 338.0 %while.2 = (s32[]{:T(128)}, f32[4,32,2,128]{3,2,1,0:T(2,128)S(1)}, f32[4,32,2,128]{3,2,1,0:T(2,128)S(1)}, s32[4,32]{1,0:T(4,128)S(1)}, f32[14,160,128]{2,0,1:T(8...) while((s32[]{:T(128)}, f32[4,32,2,128]{3,2,1,0:T(2,128)S(1)}, ...), condition=%wide.region_1.2_spmd, body=%wide.region_0.1_spmd.sunk | while | flops 321292512 | bytes 6335085 | solution.py:71
  171.1 3.8 fusion.536
  174.9 5.1 %fusion.517 = f32[32,2,128]{2,1,0:T(2,128)S(1)} fusion(f32[32,128]{1,0:T(8,128)S(1)} %get-tuple-element.250, f32[32,128]{1,0:T(8,128)S(1)} %get-tuple-element.252, f32[32,128]{1,0:T(8,128)S(1)} %get-tuple-element.253, f32[32,128]{1,0:T(8,128)S(1)} %get-tuple-element.254, f32[32,128]{1,0:T(8,128)S(1)} %get-tuple-element.255, ...), kind=kOutput, calls=%fused_computation.18.clone.1 | convolution fusion | flops 17833984 | bytes 180224 | tf_op jit(solution)/shard_map/while/body/eval_jaxpr/gab,grb->gra/dot_general | solution.py:41
  180.0 5.1 %fusion.518 = f32[32,2,128]{2,1,0:T(2,128)S(1)} fusion(f32[32,2,128]{2,1,0:T(2,128)S(1)} %fusion.517, f32[32,128]{1,0:T(8,128)S(1)} %get-tuple-element.258, f32[32,128]{1,0:T(8,128)S(1)} %get-tuple-element.259, f32[32,128]{1,0:T(8,128)S(1)} %get-tuple-element.260, f32[32,128]{1,0:T(8,128)S(1)} %get-tuple-element.252, ...), kind=kOutput, calls=%fused_computation.69.clone.1 | convolution fusion | flops 17842176 | bytes 212992 | tf_op jit(solution)/shard_map/while/body/eval_jaxpr/gab,grb->gra/dot_general | solution.py:41
  185.2 5.1 %fusion.520 = f32[32,2,128]{2,1,0:T(2,128)S(1)} fusion(f32[32,2,128]{2,1,0:T(2,128)S(1)} %fusion.518, f32[32,128]{1,0:T(8,128)S(1)} %get-tuple-element.262, f32[32,128]{1,0:T(8,128)S(1)} %get-tuple-element.263, f32[32,128]{1,0:T(8,128)S(1)} %get-tuple-element.264, f32[32,128]{1,0:T(8,128)S(1)} %get-tuple-element.252, ...), kind=kOutput, calls=%fused_computation.66.clone.1 | convolution fusion | flops 17850368 | bytes 229376 | tf_op jit(solution)/shard_map/while/body/eval_jaxpr/gab,grb->gra/dot_general | solution.py:41
  190.3 5.1 %fusion.521 = f32[32,2,128]{2,1,0:T(2,128)S(1)} fusion(f32[32,2,128]{2,1,0:T(2,128)S(1)} %fusion.520, f32[32,128]{1,0:T(8,128)S(1)} %get-tuple-element.267, f32[32,128]{1,0:T(8,128)S(1)} %get-tuple-element.268, f32[32,128]{1,0:T(8,128)S(1)} %get-tuple-element.269, f32[32,128]{1,0:T(8,128)S(1)} %get-tuple-element.250, ...), kind=kOutput, calls=%fused_computation.62.clone.1 | convolution fusion | flops 17850368 | bytes 229376 | tf_op jit(solution)/shard_map/while/body/eval_jaxpr/gab,grb->gra/dot_general | solution.py:41
  195.4 5.1 %fusion.522 = f32[32,2,128]{2,1,0:T(2,128)S(1)} fusion(f32[32,2,128]{2,1,0:T(2,128)S(1)} %fusion.521, f32[32,128]{1,0:T(8,128)S(1)} %get-tuple-element.267, f32[32,128]{1,0:T(8,128)S(1)} %get-tuple-element.268, f32[32,128]{1,0:T(8,128)S(1)} %get-tuple-element.269, f32[32,128]{1,0:T(8,128)S(1)} %get-tuple-element.258, ...), kind=kOutput, calls=%fused_computation.58.clone.1 | convolution fusion | flops 17850368 | bytes 229376 | tf_op jit(solution)/shard_map/while/body/eval_jaxpr/gab,grb->gra/dot_general | solution.py:41
  200.5 5.1 %fusion.523 = f32[32,2,128]{2,1,0:T(2,128)S(1)} fusion(f32[32,2,128]{2,1,0:T(2,128)S(1)} %fusion.522, f32[32,128]{1,0:T(8,128)S(1)} %get-tuple-element.267, f32[32,128]{1,0:T(8,128)S(1)} %get-tuple-element.268, f32[32,128]{1,0:T(8,128)S(1)} %get-tuple-element.269, f32[32,128]{1,0:T(8,128)S(1)} %get-tuple-element.262, ...), kind=kOutput, calls=%fused_computation.54.clone.1 | convolution fusion | flops 17850368 | bytes 229376 | tf_op jit(solution)/shard_map/while/body/eval_jaxpr/gab,grb->gra/dot_general | solution.py:41
  205.6 5.1 %fusion.524 = f32[32,2,128]{2,1,0:T(2,128)S(1)} fusion(f32[32,2,128]{2,1,0:T(2,128)S(1)} %fusion.523, f32[32,128]{1,0:T(8,128)S(1)} %get-tuple-element.271, f32[32,128]{1,0:T(8,128)S(1)} %get-tuple-element.272, f32[32,128]{1,0:T(8,128)S(1)} %get-tuple-element.273, f32[32,128]{1,0:T(8,128)S(1)} %get-tuple-element.250, ...), kind=kOutput, calls=%fused_computation.50.clone.1 | convolution fusion | flops 17850368 | bytes 229376 | tf_op jit(solution)/shard_map/while/body/eval_jaxpr/gab,grb->gra/dot_general | solution.py:41
  210.7 5.1 %fusion.525 = f32[32,2,128]{2,1,0:T(2,128)S(1)} fusion(f32[32,2,128]{2,1,0:T(2,128)S(1)} %fusion.524, f32[32,128]{1,0:T(8,128)S(1)} %get-tuple-element.271, f32[32,128]{1,0:T(8,128)S(1)} %get-tuple-element.272, f32[32,128]{1,0:T(8,128)S(1)} %get-tuple-element.273, f32[32,128]{1,0:T(8,128)S(1)} %get-tuple-element.258, ...), kind=kOutput, calls=%fused_computation.46.clone.1 | convolution fusion | flops 17850368 | bytes 229376 | tf_op jit(solution)/shard_map/while/body/eval_jaxpr/gab,grb->gra/dot_general | solution.py:41
  215.8 5.1 %fusion.527 = f32[4,32,2,128]{3,2,1,0:T(2,128)S(1)} fusion(f32[4,32,2,128]{3,2,1,0:T(2,128)S(1)} %get-tuple-element.287, s32[]{:T(128)} %get-tuple-element.286, f32[32,2,128]{2,1,0:T(2,128)S(1)} %fusion.525, f32[32,128]{1,0:T(8,128)S(1)} %get-tuple-element.271, f32[32,128]{1,0:T(8,128)S(1)} %get-tuple-element.272, ...), kind=kOutput, calls=%fused_computation.39.clone.1 | convolution fusion | flops 17858560 | bytes 229892 | tf_op jit(solution)/shard_map/while/body/eval_jaxpr/gab,grb->gra/dot_general | solution.py:41
  233.8 3.8 fusion.531
  248.9 3.8 fusion.535
  252.7 3.8 fusion.536
  256.5 5.1 %fusion.517 = f32[32,2,128]{2,1,0:T(2,128)S(1)} fusion(f32[32,128]{1,0:T(8,128)S(1)} %get-tuple-element.250, f32[32,128]{1,0:T(8,128)S(1)} %get-tuple-element.252, f32[32,128]{1,0:T(8,128)S(1)} %get-tuple-element.253, f32[32,128]{1,0:T(8,128)S(1)} %get-tuple-element.254, f32[32,128]{1,0:T(8,128)S(1)} %get-tuple-element.255, ...), kind=kOutput, calls=%fused_computation.18.clone.1 | convolution fusion | flops 17833984 | bytes 180224 | tf_op jit(solution)/shard_map/while/body/eval_jaxpr/gab,grb->gra/dot_general | solution.py:41
  261.6 5.1 %fusion.518 = f32[32,2,128]{2,1,0:T(2,128)S(1)} fusion(f32[32,2,128]{2,1,0:T(2,128)S(1)} %fusion.517, f32[32,128]{1,0:T(8,128)S(1)} %get-tuple-element.258, f32[32,128]{1,0:T(8,128)S(1)} %get-tuple-element.259, f32[32,128]{1,0:T(8,128)S(1)} %get-tuple-element.260, f32[32,128]{1,0:T(8,128)S(1)} %get-tuple-element.252, ...), kind=kOutput, calls=%fused_computation.69.clone.1 | convolution fusion | flops 17842176 | bytes 212992 | tf_op jit(solution)/shard_map/while/body/eval_jaxpr/gab,grb->gra/dot_general | solution.py:41
  266.7 5.1 %fusion.520 = f32[32,2,128]{2,1,0:T(2,128)S(1)} fusion(f32[32,2,128]{2,1,0:T(2,128)S(1)} %fusion.518, f32[32,128]{1,0:T(8,128)S(1)} %get-tuple-element.262, f32[32,128]{1,0:T(8,128)S(1)} %get-tuple-element.263, f32[32,128]{1,0:T(8,128)S(1)} %get-tuple-element.264, f32[32,128]{1,0:T(8,128)S(1)} %get-tuple-element.252, ...), kind=kOutput, calls=%fused_computation.66.clone.1 | convolution fusion | flops 17850368 | bytes 229376 | tf_op jit(solution)/shard_map/while/body/eval_jaxpr/gab,grb->gra/dot_general | solution.py:41
  271.8 5.1 %fusion.521 = f32[32,2,128]{2,1,0:T(2,128)S(1)} fusion(f32[32,2,128]{2,1,0:T(2,128)S(1)} %fusion.520, f32[32,128]{1,0:T(8,128)S(1)} %get-tuple-element.267, f32[32,128]{1,0:T(8,128)S(1)} %get-tuple-element.268, f32[32,128]{1,0:T(8,128)S(1)} %get-tuple-element.269, f32[32,128]{1,0:T(8,128)S(1)} %get-tuple-element.250, ...), kind=kOutput, calls=%fused_computation.62.clone.1 | convolution fusion | flops 17850368 | bytes 229376 | tf_op jit(solution)/shard_map/while/body/eval_jaxpr/gab,grb->gra/dot_general | solution.py:41
  276.9 5.1 %fusion.522 = f32[32,2,128]{2,1,0:T(2,128)S(1)} fusion(f32[32,2,128]{2,1,0:T(2,128)S(1)} %fusion.521, f32[32,128]{1,0:T(8,128)S(1)} %get-tuple-element.267, f32[32,128]{1,0:T(8,128)S(1)} %get-tuple-element.268, f32[32,128]{1,0:T(8,128)S(1)} %get-tuple-element.269, f32[32,128]{1,0:T(8,128)S(1)} %get-tuple-element.258, ...), kind=kOutput, calls=%fused_computation.58.clone.1 | convolution fusion | flops 17850368 | bytes 229376 | tf_op jit(solution)/shard_map/while/body/eval_jaxpr/gab,grb->gra/dot_general | solution.py:41
  282.1 5.1 %fusion.523 = f32[32,2,128]{2,1,0:T(2,128)S(1)} fusion(f32[32,2,128]{2,1,0:T(2,128)S(1)} %fusion.522, f32[32,128]{1,0:T(8,128)S(1)} %get-tuple-element.267, f32[32,128]{1,0:T(8,128)S(1)} %get-tuple-element.268, f32[32,128]{1,0:T(8,128)S(1)} %get-tuple-element.269, f32[32,128]{1,0:T(8,128)S(1)} %get-tuple-element.262, ...), kind=kOutput, calls=%fused_computation.54.clone.1 | convolution fusion | flops 17850368 | bytes 229376 | tf_op jit(solution)/shard_map/while/body/eval_jaxpr/gab,grb->gra/dot_general | solution.py:41
  287.2 5.1 %fusion.524 = f32[32,2,128]{2,1,0:T(2,128)S(1)} fusion(f32[32,2,128]{2,1,0:T(2,128)S(1)} %fusion.523, f32[32,128]{1,0:T(8,128)S(1)} %get-tuple-element.271, f32[32,128]{1,0:T(8,128)S(1)} %get-tuple-element.272, f32[32,128]{1,0:T(8,128)S(1)} %get-tuple-element.273, f32[32,128]{1,0:T(8,128)S(1)} %get-tuple-element.250, ...), kind=kOutput, calls=%fused_computation.50.clone.1 | convolution fusion | flops 17850368 | bytes 229376 | tf_op jit(solution)/shard_map/while/body/eval_jaxpr/gab,grb->gra/dot_general | solution.py:41
  292.3 5.1 %fusion.525 = f32[32,2,128]{2,1,0:T(2,128)S(1)} fusion(f32[32,2,128]{2,1,0:T(2,128)S(1)} %fusion.524, f32[32,128]{1,0:T(8,128)S(1)} %get-tuple-element.271, f32[32,128]{1,0:T(8,128)S(1)} %get-tuple-element.272, f32[32,128]{1,0:T(8,128)S(1)} %get-tuple-element.273, f32[32,128]{1,0:T(8,128)S(1)} %get-tuple-element.258, ...), kind=kOutput, calls=%fused_computation.46.clone.1 | convolution fusion | flops 17850368 | bytes 229376 | tf_op jit(solution)/shard_map/while/body/eval_jaxpr/gab,grb->gra/dot_general | solution.py:41
  297.4 5.1 %fusion.527 = f32[4,32,2,128]{3,2,1,0:T(2,128)S(1)} fusion(f32[4,32,2,128]{3,2,1,0:T(2,128)S(1)} %get-tuple-element.287, s32[]{:T(128)} %get-tuple-element.286, f32[32,2,128]{2,1,0:T(2,128)S(1)} %fusion.525, f32[32,128]{1,0:T(8,128)S(1)} %get-tuple-element.271, f32[32,128]{1,0:T(8,128)S(1)} %get-tuple-element.272, ...), kind=kOutput, calls=%fused_computation.39.clone.1 | convolution fusion | flops 17858560 | bytes 229892 | tf_op jit(solution)/shard_map/while/body/eval_jaxpr/gab,grb->gra/dot_general | solution.py:41
  315.4 3.8 fusion.531
  334.2 3.8 fusion.536
  338.1 5.1 %fusion.517 = f32[32,2,128]{2,1,0:T(2,128)S(1)} fusion(f32[32,128]{1,0:T(8,128)S(1)} %get-tuple-element.250, f32[32,128]{1,0:T(8,128)S(1)} %get-tuple-element.252, f32[32,128]{1,0:T(8,128)S(1)} %get-tuple-element.253, f32[32,128]{1,0:T(8,128)S(1)} %get-tuple-element.254, f32[32,128]{1,0:T(8,128)S(1)} %get-tuple-element.255, ...), kind=kOutput, calls=%fused_computation.18.clone.1 | convolution fusion | flops 17833984 | bytes 180224 | tf_op jit(solution)/shard_map/while/body/eval_jaxpr/gab,grb->gra/dot_general | solution.py:41
  343.2 5.1 %fusion.518 = f32[32,2,128]{2,1,0:T(2,128)S(1)} fusion(f32[32,2,128]{2,1,0:T(2,128)S(1)} %fusion.517, f32[32,128]{1,0:T(8,128)S(1)} %get-tuple-element.258, f32[32,128]{1,0:T(8,128)S(1)} %get-tuple-element.259, f32[32,128]{1,0:T(8,128)S(1)} %get-tuple-element.260, f32[32,128]{1,0:T(8,128)S(1)} %get-tuple-element.252, ...), kind=kOutput, calls=%fused_computation.69.clone.1 | convolution fusion | flops 17842176 | bytes 212992 | tf_op jit(solution)/shard_map/while/body/eval_jaxpr/gab,grb->gra/dot_general | solution.py:41
  348.3 5.1 %fusion.520 = f32[32,2,128]{2,1,0:T(2,128)S(1)} fusion(f32[32,2,128]{2,1,0:T(2,128)S(1)} %fusion.518, f32[32,128]{1,0:T(8,128)S(1)} %get-tuple-element.262, f32[32,128]{1,0:T(8,128)S(1)} %get-tuple-element.263, f32[32,128]{1,0:T(8,128)S(1)} %get-tuple-element.264, f32[32,128]{1,0:T(8,128)S(1)} %get-tuple-element.252, ...), kind=kOutput, calls=%fused_computation.66.clone.1 | convolution fusion | flops 17850368 | bytes 229376 | tf_op jit(solution)/shard_map/while/body/eval_jaxpr/gab,grb->gra/dot_general | solution.py:41
  353.4 5.1 %fusion.521 = f32[32,2,128]{2,1,0:T(2,128)S(1)} fusion(f32[32,2,128]{2,1,0:T(2,128)S(1)} %fusion.520, f32[32,128]{1,0:T(8,128)S(1)} %get-tuple-element.267, f32[32,128]{1,0:T(8,128)S(1)} %get-tuple-element.268, f32[32,128]{1,0:T(8,128)S(1)} %get-tuple-element.269, f32[32,128]{1,0:T(8,128)S(1)} %get-tuple-element.250, ...), kind=kOutput, calls=%fused_computation.62.clone.1 | convolution fusion | flops 17850368 | bytes 229376 | tf_op jit(solution)/shard_map/while/body/eval_jaxpr/gab,grb->gra/dot_general | solution.py:41
  358.5 5.1 %fusion.522 = f32[32,2,128]{2,1,0:T(2,128)S(1)} fusion(f32[32,2,128]{2,1,0:T(2,128)S(1)} %fusion.521, f32[32,128]{1,0:T(8,128)S(1)} %get-tuple-element.267, f32[32,128]{1,0:T(8,128)S(1)} %get-tuple-element.268, f32[32,128]{1,0:T(8,128)S(1)} %get-tuple-element.269, f32[32,128]{1,0:T(8,128)S(1)} %get-tuple-element.258, ...), kind=kOutput, calls=%fused_computation.58.clone.1 | convolution fusion | flops 17850368 | bytes 229376 | tf_op jit(solution)/shard_map/while/body/eval_jaxpr/gab,grb->gra/dot_general | solution.py:41
  363.6 5.1 %fusion.523 = f32[32,2,128]{2,1,0:T(2,128)S(1)} fusion(f32[32,2,128]{2,1,0:T(2,128)S(1)} %fusion.522, f32[32,128]{1,0:T(8,128)S(1)} %get-tuple-element.267, f32[32,128]{1,0:T(8,128)S(1)} %get-tuple-element.268, f32[32,128]{1,0:T(8,128)S(1)} %get-tuple-element.269, f32[32,128]{1,0:T(8,128)S(1)} %get-tuple-element.262, ...), kind=kOutput, calls=%fused_computation.54.clone.1 | convolution fusion | flops 17850368 | bytes 229376 | tf_op jit(solution)/shard_map/while/body/eval_jaxpr/gab,grb->gra/dot_general | solution.py:41
  368.7 5.1 %fusion.524 = f32[32,2,128]{2,1,0:T(2,128)S(1)} fusion(f32[32,2,128]{2,1,0:T(2,128)S(1)} %fusion.523, f32[32,128]{1,0:T(8,128)S(1)} %get-tuple-element.271, f32[32,128]{1,0:T(8,128)S(1)} %get-tuple-element.272, f32[32,128]{1,0:T(8,128)S(1)} %get-tuple-element.273, f32[32,128]{1,0:T(8,128)S(1)} %get-tuple-element.250, ...), kind=kOutput, calls=%fused_computation.50.clone.1 | convolution fusion | flops 17850368 | bytes 229376 | tf_op jit(solution)/shard_map/while/body/eval_jaxpr/gab,grb->gra/dot_general | solution.py:41
  373.9 5.1 %fusion.525 = f32[32,2,128]{2,1,0:T(2,128)S(1)} fusion(f32[32,2,128]{2,1,0:T(2,128)S(1)} %fusion.524, f32[32,128]{1,0:T(8,128)S(1)} %get-tuple-element.271, f32[32,128]{1,0:T(8,128)S(1)} %get-tuple-element.272, f32[32,128]{1,0:T(8,128)S(1)} %get-tuple-element.273, f32[32,128]{1,0:T(8,128)S(1)} %get-tuple-element.258, ...), kind=kOutput, calls=%fused_computation.46.clone.1 | convolution fusion | flops 17850368 | bytes 229376 | tf_op jit(solution)/shard_map/while/body/eval_jaxpr/gab,grb->gra/dot_general | solution.py:41
  379.0 5.1 %fusion.527 = f32[4,32,2,128]{3,2,1,0:T(2,128)S(1)} fusion(f32[4,32,2,128]{3,2,1,0:T(2,128)S(1)} %get-tuple-element.287, s32[]{:T(128)} %get-tuple-element.286, f32[32,2,128]{2,1,0:T(2,128)S(1)} %fusion.525, f32[32,128]{1,0:T(8,128)S(1)} %get-tuple-element.271, f32[32,128]{1,0:T(8,128)S(1)} %get-tuple-element.272, ...), kind=kOutput, calls=%fused_computation.39.clone.1 | convolution fusion | flops 17858560 | bytes 229892 | tf_op jit(solution)/shard_map/while/body/eval_jaxpr/gab,grb->gra/dot_general | solution.py:41
  408.3 3.8 fusion.534
  415.8 3.8 fusion.536
  419.6 5.1 %fusion.517 = f32[32,2,128]{2,1,0:T(2,128)S(1)} fusion(f32[32,128]{1,0:T(8,128)S(1)} %get-tuple-element.250, f32[32,128]{1,0:T(8,128)S(1)} %get-tuple-element.252, f32[32,128]{1,0:T(8,128)S(1)} %get-tuple-element.253, f32[32,128]{1,0:T(8,128)S(1)} %get-tuple-element.254, f32[32,128]{1,0:T(8,128)S(1)} %get-tuple-element.255, ...), kind=kOutput, calls=%fused_computation.18.clone.1 | convolution fusion | flops 17833984 | bytes 180224 | tf_op jit(solution)/shard_map/while/body/eval_jaxpr/gab,grb->gra/dot_general | solution.py:41
  424.7 5.1 %fusion.518 = f32[32,2,128]{2,1,0:T(2,128)S(1)} fusion(f32[32,2,128]{2,1,0:T(2,128)S(1)} %fusion.517, f32[32,128]{1,0:T(8,128)S(1)} %get-tuple-element.258, f32[32,128]{1,0:T(8,128)S(1)} %get-tuple-element.259, f32[32,128]{1,0:T(8,128)S(1)} %get-tuple-element.260, f32[32,128]{1,0:T(8,128)S(1)} %get-tuple-element.252, ...), kind=kOutput, calls=%fused_computation.69.clone.1 | convolution fusion | flops 17842176 | bytes 212992 | tf_op jit(solution)/shard_map/while/body/eval_jaxpr/gab,grb->gra/dot_general | solution.py:41
  429.9 5.1 %fusion.520 = f32[32,2,128]{2,1,0:T(2,128)S(1)} fusion(f32[32,2,128]{2,1,0:T(2,128)S(1)} %fusion.518, f32[32,128]{1,0:T(8,128)S(1)} %get-tuple-element.262, f32[32,128]{1,0:T(8,128)S(1)} %get-tuple-element.263, f32[32,128]{1,0:T(8,128)S(1)} %get-tuple-element.264, f32[32,128]{1,0:T(8,128)S(1)} %get-tuple-element.252, ...), kind=kOutput, calls=%fused_computation.66.clone.1 | convolution fusion | flops 17850368 | bytes 229376 | tf_op jit(solution)/shard_map/while/body/eval_jaxpr/gab,grb->gra/dot_general | solution.py:41
  435.0 5.1 %fusion.521 = f32[32,2,128]{2,1,0:T(2,128)S(1)} fusion(f32[32,2,128]{2,1,0:T(2,128)S(1)} %fusion.520, f32[32,128]{1,0:T(8,128)S(1)} %get-tuple-element.267, f32[32,128]{1,0:T(8,128)S(1)} %get-tuple-element.268, f32[32,128]{1,0:T(8,128)S(1)} %get-tuple-element.269, f32[32,128]{1,0:T(8,128)S(1)} %get-tuple-element.250, ...), kind=kOutput, calls=%fused_computation.62.clone.1 | convolution fusion | flops 17850368 | bytes 229376 | tf_op jit(solution)/shard_map/while/body/eval_jaxpr/gab,grb->gra/dot_general | solution.py:41
  440.1 5.1 %fusion.522 = f32[32,2,128]{2,1,0:T(2,128)S(1)} fusion(f32[32,2,128]{2,1,0:T(2,128)S(1)} %fusion.521, f32[32,128]{1,0:T(8,128)S(1)} %get-tuple-element.267, f32[32,128]{1,0:T(8,128)S(1)} %get-tuple-element.268, f32[32,128]{1,0:T(8,128)S(1)} %get-tuple-element.269, f32[32,128]{1,0:T(8,128)S(1)} %get-tuple-element.258, ...), kind=kOutput, calls=%fused_computation.58.clone.1 | convolution fusion | flops 17850368 | bytes 229376 | tf_op jit(solution)/shard_map/while/body/eval_jaxpr/gab,grb->gra/dot_general | solution.py:41
  445.2 5.1 %fusion.523 = f32[32,2,128]{2,1,0:T(2,128)S(1)} fusion(f32[32,2,128]{2,1,0:T(2,128)S(1)} %fusion.522, f32[32,128]{1,0:T(8,128)S(1)} %get-tuple-element.267, f32[32,128]{1,0:T(8,128)S(1)} %get-tuple-element.268, f32[32,128]{1,0:T(8,128)S(1)} %get-tuple-element.269, f32[32,128]{1,0:T(8,128)S(1)} %get-tuple-element.262, ...), kind=kOutput, calls=%fused_computation.54.clone.1 | convolution fusion | flops 17850368 | bytes 229376 | tf_op jit(solution)/shard_map/while/body/eval_jaxpr/gab,grb->gra/dot_general | solution.py:41
  450.3 5.1 %fusion.524 = f32[32,2,128]{2,1,0:T(2,128)S(1)} fusion(f32[32,2,128]{2,1,0:T(2,128)S(1)} %fusion.523, f32[32,128]{1,0:T(8,128)S(1)} %get-tuple-element.271, f32[32,128]{1,0:T(8,128)S(1)} %get-tuple-element.272, f32[32,128]{1,0:T(8,128)S(1)} %get-tuple-element.273, f32[32,128]{1,0:T(8,128)S(1)} %get-tuple-element.250, ...), kind=kOutput, calls=%fused_computation.50.clone.1 | convolution fusion | flops 17850368 | bytes 229376 | tf_op jit(solution)/shard_map/while/body/eval_jaxpr/gab,grb->gra/dot_general | solution.py:41
  455.4 5.1 %fusion.525 = f32[32,2,128]{2,1,0:T(2,128)S(1)} fusion(f32[32,2,128]{2,1,0:T(2,128)S(1)} %fusion.524, f32[32,128]{1,0:T(8,128)S(1)} %get-tuple-element.271, f32[32,128]{1,0:T(8,128)S(1)} %get-tuple-element.272, f32[32,128]{1,0:T(8,128)S(1)} %get-tuple-element.273, f32[32,128]{1,0:T(8,128)S(1)} %get-tuple-element.258, ...), kind=kOutput, calls=%fused_computation.46.clone.1 | convolution fusion | flops 17850368 | bytes 229376 | tf_op jit(solution)/shard_map/while/body/eval_jaxpr/gab,grb->gra/dot_general | solution.py:41
  460.5 5.1 %fusion.527 = f32[4,32,2,128]{3,2,1,0:T(2,128)S(1)} fusion(f32[4,32,2,128]{3,2,1,0:T(2,128)S(1)} %get-tuple-element.287, s32[]{:T(128)} %get-tuple-element.286, f32[32,2,128]{2,1,0:T(2,128)S(1)} %fusion.525, f32[32,128]{1,0:T(8,128)S(1)} %get-tuple-element.271, f32[32,128]{1,0:T(8,128)S(1)} %get-tuple-element.272, ...), kind=kOutput, calls=%fused_computation.39.clone.1 | convolution fusion | flops 17858560 | bytes 229892 | tf_op jit(solution)/shard_map/while/body/eval_jaxpr/gab,grb->gra/dot_general | solution.py:41
  465.8 5.0 scatter_fusion
  470.8 4.9 scatter_fusion.1
  477.9 7.1 %collective-permute-start.5 = (f32[2,4096]{1,0:T(2,128)S(1)}, f32[2,4096]{1,0:T(2,128)S(1)}, u32[]{:S(2)}, u32[]{:S(2)}) collective-permute-start(f32[2,4096]{1,0:T(2,128)S(1)} %get-tuple-element.147), channel_id=1, source_target_pairs={{1,0},{2,1},{3,2},{4,3},{5,4},{6,5},{7,6},{8,7},{9,8},{10,9},{11,1... | collective-permute-start | bytes 98312 | tf_op jit(solution)/shard_map/ppermute | solution.py:18
  (147 shorter events, 161.9 us)
Async XLA Ops:
  6.5 27.4 %copy-start.1 = (s32[3,32]{1,0:T(4,128)S(1)}, s32[3,32]{1,0:T(4,128)}, u32[]{:S(2)}) copy-start(s32[3,32]{1,0:T(4,128)} %param.11) | copy-start | bytes 1156
  6.5 483.5 %reduce-scatter.4.cloned.1.call-start = ((), (), s32[]{:S(2)}) async-start(), calls=%async_computation.1 | async-start | bytes 10485760
  8.5 118.0 %collective-permute-start = (f32[14,4096]{1,0:T(8,128)S(1)}, f32[14,4096]{1,0:T(8,128)S(1)}, u32[]{:S(2)}, u32[]{:S(2)}) collective-permute-start(f32[14,4096]{1,0:T(8,128)S(1)} %pad_maximum_fusion), channel_id=1, source_target_pairs={{0,2},{1,3},{2,4},{3,5},{4,6},{5,7},{6,8},{7,9},{8,10},{9,11},{10,... | collective-permute-start | bytes 688136 | tf_op jit(solution)/shard_map/ppermute | solution.py:18
  11.6 114.9 %collective-permute-start.1 = (f32[14,4096]{1,0:T(8,128)S(1)}, f32[14,4096]{1,0:T(8,128)S(1)}, u32[]{:S(2)}, u32[]{:S(2)}) collective-permute-start(f32[14,4096]{1,0:T(8,128)S(1)} %pad_maximum_fusion), channel_id=1, source_target_pairs={{0,1},{1,2},{2,3},{3,4},{4,5},{5,6},{6,7},{7,8},{8,9},{9,10},{10,1... | collective-permute-start | bytes 688136 | tf_op jit(solution)/shard_map/ppermute | solution.py:18
  15.6 111.0 %collective-permute-start.2 = (f32[14,4096]{1,0:T(8,128)S(1)}, f32[14,4096]{1,0:T(8,128)S(1)}, u32[]{:S(2)}, u32[]{:S(2)}) collective-permute-start(f32[14,4096]{1,0:T(8,128)S(1)} %pad_maximum_fusion), channel_id=1, source_target_pairs={{1,0},{2,1},{3,2},{4,3},{5,4},{6,5},{7,6},{8,7},{9,8},{10,9},{11,1... | collective-permute-start | bytes 688136 | tf_op jit(solution)/shard_map/ppermute | solution.py:18
  17.5 109.1 %collective-permute-start.3 = (f32[14,4096]{1,0:T(8,128)S(1)}, f32[14,4096]{1,0:T(8,128)S(1)}, u32[]{:S(2)}, u32[]{:S(2)}) collective-permute-start(f32[14,4096]{1,0:T(8,128)S(1)} %pad_maximum_fusion), channel_id=1, source_target_pairs={{2,0},{3,1},{4,2},{5,3},{6,4},{7,5},{8,6},{9,7},{10,8},{11,9},{12,... | collective-permute-start | bytes 688136 | tf_op jit(solution)/shard_map/ppermute | solution.py:18
  124.9 0.7 copy-start
  127.7 338.1 %copy-start.3 = (s32[128]{0:T(128)S(1)}, s32[128]{0:T(128)}, u32[]{:S(2)}) copy-start(s32[128]{0:T(128)} %get-tuple-element.167) | copy-start | bytes 1540
  127.7 343.1 %copy-start.2 = (s32[128]{0:T(128)S(1)}, s32[128]{0:T(128)}, u32[]{:S(2)}) copy-start(s32[128]{0:T(128)} %get-tuple-element.166) | copy-start | bytes 1540
  475.7 16.5 %collective-permute-start.4 = (f32[2,4096]{1,0:T(2,128)S(1)}, f32[2,4096]{1,0:T(2,128)S(1)}, u32[]{:S(2)}, u32[]{:S(2)}) collective-permute-start(f32[2,4096]{1,0:T(2,128)S(1)} %get-tuple-element.144), channel_id=1, source_target_pairs={{2,0},{3,1},{4,2},{5,3},{6,4},{7,5},{8,6},{9,7},{10,8},{11,9},{12,... | collective-permute-start | bytes 98312 | tf_op jit(solution)/shard_map/ppermute | solution.py:18
  477.9 14.4 %collective-permute-start.5 = (f32[2,4096]{1,0:T(2,128)S(1)}, f32[2,4096]{1,0:T(2,128)S(1)}, u32[]{:S(2)}, u32[]{:S(2)}) collective-permute-start(f32[2,4096]{1,0:T(2,128)S(1)} %get-tuple-element.147), channel_id=1, source_target_pairs={{1,0},{2,1},{3,2},{4,3},{5,4},{6,5},{7,6},{8,7},{9,8},{10,9},{11,1... | collective-permute-start | bytes 98312 | tf_op jit(solution)/shard_map/ppermute | solution.py:18
  485.0 7.3 %collective-permute-start.6 = (f32[2,4096]{1,0:T(2,128)S(1)}, f32[2,4096]{1,0:T(2,128)S(1)}, u32[]{:S(2)}, u32[]{:S(2)}) collective-permute-start(f32[2,4096]{1,0:T(2,128)S(1)} %get-tuple-element.146), channel_id=1, source_target_pairs={{0,1},{1,2},{2,3},{3,4},{4,5},{5,6},{6,7},{7,8},{8,9},{9,10},{10,1... | collective-permute-start | bytes 98312 | tf_op jit(solution)/shard_map/ppermute | solution.py:18
  488.0 7.2 %collective-permute-start.7 = (f32[2,4096]{1,0:T(2,128)S(1)}, f32[2,4096]{1,0:T(2,128)S(1)}, u32[]{:S(2)}, u32[]{:S(2)}) collective-permute-start(f32[2,4096]{1,0:T(2,128)S(1)} %get-tuple-element.145), channel_id=1, source_target_pairs={{0,2},{1,3},{2,4},{3,5},{4,6},{5,7},{6,8},{7,9},{8,10},{9,11},{10,... | collective-permute-start | bytes 98312 | tf_op jit(solution)/shard_map/ppermute | solution.py:18
Sparse Core Ops, SparseCore 0:
  125.0 82.2 reduce-scatter.3
where the time goes:
time: 507 us; the launch traced here: 503 us
  matrix products  400 us (79%)
  starting transfers between devices  27.5 us (5%)
  local copies, waits for them, and re-layouts  18.1 us (4%)
  other arithmetic  15.5 us (3%)
  between operations  14.1 us (3%)
  loops' own time  12.5 us (2%)
  blocking collectives  12.2 us (2%)
    dot_general x45, matrix products, pair_terms(): jnp.einsum('gab,grb->gra', kernel_tile, load_b, precision=lax.Precision.H...  230 us
    dot_general x45, matrix products, pair_terms(): jnp.einsum('gab,gra->grb', kernel_tile, load_a, precision=lax.Precision.H...  170 us
    ppermute x8, starting transfers between devices, passed_along(): return lax.ppermute(block, axis, route)  27.5 us
    another operation x1, loops' own time, accumulate(): terms_a, terms_b = lax.map(one_group, items)  12.5 us
    all_gather x1, blocking collectives, facing_part(): facing_table = lax.all_gather(local_table, 'section', axis=1, tiled=True)  12.2 us
  transfers between devices with their start and end apart: 9, of which 1 were waited for; matrix products, arithmetic and copies ran while one was open for 86% of the time, Pallas kernels for 0%

commit v1 on v0

v1 whole, which is shorter than its diff:
```python
import functools
import math

import jax
import jax.numpy as jnp
from jax import lax
from jax.experimental import pallas as pl
from jax.experimental.pallas import tpu as pltpu
from jax.sharding import PartitionSpec as P

CL = 128
QUAD = 3
DEPTH = 48
UNROLL = 4

smoothing = 0.02
green_scale = 0.25 / math.pi
f32 = jnp.float32
bf16 = jnp.bfloat16


def rounded(x, magic):
    return (x + magic) - magic


def row_ids():
    return lax.broadcasted_iota(jnp.int32, (8, CL), 0)


def parts_of(tile, row_limit):
    rows = row_ids()
    live = jnp.logical_and(lax.rem(rows, 4) < 3, rows < row_limit)
    x = jnp.where(live, tile, 0.0)
    high = rounded(x, 49152.0)
    rest = x - high
    mid = rounded(rest, 96.0)
    low = rounded(rest - mid, 0.1875)
    rest = mid + low
    sq_high = high * high
    sq_rest = rest * (high + high + rest)

    def row_sum(v):
        u = v + pltpu.roll(v, 7, 0)
        return u + pltpu.roll(u, 6, 0)

    return high, mid, low, row_sum(sq_high), row_sum(sq_rest)


def square_parts(sum_high, sum_rest):
    rows = row_ids()
    upper = rows < 4
    v = jnp.where(upper, sum_high, sum_rest)
    one = rounded(v, jnp.where(upper, 196608.0, 768.0))
    rest = v - one
    two = rounded(rest, jnp.where(upper, 768.0, 3.0))
    three = rest - two
    place = lax.rem(rows, 4)
    return jnp.where(place == 0, one, jnp.where(place == 1, two, jnp.where(place == 2, three, 0.0)))


def point_features(tile0, tile1):
    h0, m0, l0, sh0, sr0 = parts_of(tile0, 8)
    h1, m1, l1, sh1, sr1 = parts_of(tile1, 3)

    def spread(v, row):
        return jnp.broadcast_to(v[row : row + 1], (8, CL))

    turn = lambda v: pltpu.roll(v, 4, 0)
    return (
        (h0, m0, l0, turn(l0), spread(sh0, 0), spread(sr0, 0)),
        (turn(h0), turn(m0), turn(l0), l0, spread(sh0, 4), spread(sr0, 4)),
        (h1, m1, l1, turn(l1), spread(sh1, 0), spread(sr1, 0)),
    )


def right_features(tile0, tile1):
    rows = row_ids()
    out = []
    for high, mid, low, low_turned, sum_high, sum_rest in point_features(tile0, tile1):
        ones = jnp.where(rows < 6, 1.0, 0.0)
        g0 = jnp.where(rows < 3, high, ones)
        g1 = square_parts(sum_high, sum_rest + smoothing * smoothing)
        g4 = jnp.where(rows < 4, mid, low_turned)
        out.append(jnp.concatenate([g0, g1, g0, g0, g4, g4], 0).astype(bf16))
    return out


def left_features(tile0, tile1):
    rows = row_ids()
    out = []
    for high, mid, low, low_turned, sum_high, sum_rest in point_features(tile0, tile1):
        sq = square_parts(sum_high, sum_rest)
        sq_high = pltpu.roll(sq, 3, 0)
        sq_rest = pltpu.roll(sq, 7, 0)
        first = rows < 3
        mids = jnp.logical_and(rows >= 3, rows < 6)
        h2 = jnp.where(first, -2.0 * high, 0.0)
        m2 = jnp.where(first, -2.0 * mid, 0.0)
        l2 = jnp.where(first, -2.0 * low, 0.0)
        b0 = jnp.where(mids, sq_high, h2)
        b1 = jnp.where(lax.rem(rows, 4) < 3, 1.0, 0.0)
        b2 = jnp.where(mids, sq_rest, m2)
        b4 = h2 + pltpu.roll(h2, 4, 0)
        b5 = m2 + pltpu.roll(m2, 4, 0)
        out.append(jnp.concatenate([b0, b1, b2, l2, b4, b5], 0))
    return out


def pair_kernel(kind, tables, clusters, *refs):
    pairs, local = refs[0], refs[1]
    others = refs[2 : 2 + tables] if kind != "local" else (local,)
    refs = refs[2 + (tables if kind != "local" else 0) :]
    out_a, out_b = refs[0], refs[1]
    todo, left, right, raw, wide_w, wide_d, acc_a, acc_b = refs[2:]
    slots = pairs.shape[1]
    cl_bits = clusters.bit_length() - 1

    def collect(t, count):
        first, second, listed = pairs[0, t], pairs[1, t], pairs[2, t]
        i = jnp.bitwise_and(first, clusters - 1)
        j = jnp.bitwise_and(second, clusters - 1)
        if kind == "gap":
            sec_bits = cl_bits + 5
            step = jnp.bitwise_and(
                lax.shift_right_logical(second, sec_bits) - lax.shift_right_logical(first, sec_bits) + 4, 3
            )
            table = step - 1
            take = listed
        else:
            step = lax.shift_right_logical(second, cl_bits) - lax.shift_right_logical(first, cl_bits)
            here = (step == 0).astype(jnp.int32)
            if kind == "local":
                table = 0
                take = listed * here
            else:
                table = jnp.where(step < 0, step + 2, step + 1)
                take = listed * (1 - here)
        twice = (first != second).astype(jnp.int32)
        todo[0, count] = i
        todo[1, count] = table * clusters + j
        todo[2, count] = 1
        todo[3, count] = twice
        return count + take

    count = lax.fori_loop(0, slots, collect, 0)
    for extra in range(UNROLL - 1):
        todo[0, count + extra] = 0
        todo[1, count + extra] = 0
        todo[2, count + extra] = 0
        todo[3, count + extra] = 0

    def prepare_left(c, carry):
        lanes = pl.ds(pl.multiple_of(c * CL, CL), CL)
        tile0, tile1 = local[0:8, lanes], local[8:16, lanes]
        weight_rows = (tile0[3:4], tile0[7:8], tile1[3:4])
        dens_rows = (tile1[4:5], tile1[5:6])
        for q, block in enumerate(left_features(tile0, tile1)):
            block = jnp.concatenate([block, jnp.zeros((CL - DEPTH, CL), f32)], 0)
            left[c, q * CL : (q + 1) * CL, :] = jnp.transpose(block).astype(bf16)
            wide_w[c, q * CL : (q + 1) * CL, :] = jnp.transpose(
                jnp.broadcast_to(weight_rows[q] * green_scale, (CL, CL))
            )
        for r in range(2):
            wide_d[c, r * CL : (r + 1) * CL, :] = jnp.transpose(jnp.broadcast_to(dens_rows[r], (CL, CL)))
        acc_a[c] = jnp.zeros((2 * CL, CL), f32)
        return carry

    lax.fori_loop(0, clusters, prepare_left, 0)

    def prepare_right(table, ref):
        def body(c, carry):
            lanes = pl.ds(pl.multiple_of(c * CL, CL), CL)
            tile0, tile1 = ref[0:8, lanes], ref[8:16, lanes]
            place = table * clusters + c
            for q, block in enumerate(right_features(tile0, tile1)):
                right[place, :, q * CL : (q + 1) * CL] = block
            raw[place, 0:8, :] = tile0
            raw[place, 8:16, :] = tile1
            acc_b[place] = jnp.zeros((16, CL), f32)
            return carry

        lax.fori_loop(0, clusters, body, 0)

    for table in range(len(others)):
        prepare_right(table, others[table])

    def tile_of(i, j):
        weight_b = (raw[j, 3:4, :], raw[j, 7:8, :], raw[j, 11:12, :])
        far = right[j]
        total = None
        for p in range(QUAD):
            near = left[i, p * CL : (p + 1) * CL, 0:DEPTH]
            dist = jnp.dot(near, far, preferred_element_type=f32)
            row = None
            for q in range(QUAD):
                term = weight_b[q] * lax.rsqrt(dist[:, q * CL : (q + 1) * CL])
                row = term if row is None else row + term
            row = row * wide_w[i, p * CL : (p + 1) * CL, :]
            total = row if total is None else total + row
        return total

    def group(g, carry):
        done = []
        for u in range(UNROLL):
            t = g * UNROLL + u
            i, j = todo[0, t], todo[1, t]
            listed, twice = todo[2, t].astype(f32), todo[3, t].astype(f32)
            tile = tile_of(i, j)
            terms_b = []
            for r in range(2):
                product = tile * wide_d[i, r * CL : (r + 1) * CL, :]
                part = product[0:8]
                for k in range(1, CL // 8):
                    part = part + product[8 * k : 8 * k + 8]
                terms_b.append(part * twice)
            done.append((i, j, listed, tile, terms_b))
        for i, j, listed, tile, terms_b in done:
            for r in range(2):
                acc_b[j, 8 * r : 8 * r + 8, :] += terms_b[r]
                acc_a[i, r * CL : (r + 1) * CL, :] += tile * (raw[j, 12 + r : 13 + r, :] * listed)
        return carry

    lax.fori_loop(0, lax.div(count + UNROLL - 1, UNROLL), group, 0)

    def finish_a(c, carry):
        lanes = pl.ds(pl.multiple_of(c * CL, CL), CL)
        value = acc_a[c]
        high = value.astype(bf16)
        low = (value - high.astype(f32)).astype(bf16)
        both = jnp.concatenate([high, low], 1)
        ones = jnp.ones((8, 2 * CL), bf16)
        sums = lax.dot_general(ones, both, (((1,), (1,)), ((), ())), preferred_element_type=f32)
        rows = [sums[0:1, 0:CL], sums[0:1, CL : 2 * CL]]
        if kind == "local":
            for r in range(2):
                rows[r] = rows[r] + jnp.sum(acc_b[c, 8 * r : 8 * r + 8, :], 0, keepdims=True)
        for r in range(2):
            out_a[r : r + 1, lanes] = rows[r]
        return carry

    lax.fori_loop(0, clusters, finish_a, 0)

    for table in range(len(others)):
        if kind == "local":
            continue

        def finish_b(c, carry):
            lanes = pl.ds(pl.multiple_of(c * CL, CL), CL)
            for r in range(2):
                out_b[table, r : r + 1, lanes] = jnp.sum(
                    acc_b[table * clusters + c, 8 * r : 8 * r + 8, :], 0, keepdims=True
                )
            return carry

        lax.fori_loop(0, clusters, finish_b, 0)
    if kind == "local":
        out_b[...] = jnp.zeros_like(out_b)


def pair_sums(kind, pairs, local, others):
    panels = local.shape[1]
    clusters = panels // CL
    tables = max(len(others), 1)
    places = tables * clusters
    whole = pl.BlockSpec(memory_space=pltpu.VMEM)
    out_b_shape = (1, 8, CL) if kind == "local" else (tables, 2, panels)
    return pl.pallas_call(
        functools.partial(pair_kernel, kind, tables, clusters),
        out_shape=[
            jax.ShapeDtypeStruct((2, panels), f32),
            jax.ShapeDtypeStruct(out_b_shape, f32),
        ],
        in_specs=[pl.BlockSpec(memory_space=pltpu.SMEM)] + [whole] * (1 + len(others)),
        out_specs=[whole, whole],
        scratch_shapes=[
            pltpu.SMEM((4, pairs.shape[1] + UNROLL), jnp.int32),
            pltpu.VMEM((clusters, QUAD * CL, CL), bf16),
            pltpu.VMEM((places, DEPTH, QUAD * CL), bf16),
            pltpu.VMEM((places, 16, CL), f32),
            pltpu.VMEM((clusters, QUAD * CL, CL), f32),
            pltpu.VMEM((clusters, 2 * CL, CL), f32),
            pltpu.VMEM((clusters, 2 * CL, CL), f32),
            pltpu.VMEM((places, 16, CL), f32),
        ],
        compiler_params=pltpu.CompilerParams(vmem_limit_bytes=56 * 1024 * 1024),
        name="pairs_" + kind,
    )(pairs, local, *others)


def pack_kernel(points, weights, density, out):
    for q in range(QUAD):
        for c in range(3):
            out[4 * q + c : 4 * q + c + 1, :] = points[c, q : q + 1, :]
        out[4 * q + 3 : 4 * q + 4, :] = weights[q : q + 1, :]
    out[12:14, :] = density[...]
    out[14:16, :] = jnp.zeros((2, out.shape[1]), f32)


def packed(points, weights, density):
    whole = pl.BlockSpec(memory_space=pltpu.VMEM)
    return pl.pallas_call(
        pack_kernel,
        out_shape=jax.ShapeDtypeStruct((16, points.shape[2]), f32),
        in_specs=[whole] * 3,
        out_specs=whole,
        name="pack",
    )(points, weights, density)


def from_offset(block, axis, offset, ring):
    size = lax.axis_size(axis)
    if ring:
        route = [((i + offset) % size, i) for i in range(size)]
    else:
        route = [(i + offset, i) for i in range(size) if 0 <= i + offset < size]
    return lax.ppermute(block, axis, route)


near_offsets = (-2, -1, 1, 2)
gap_offsets = (1, 2, 3)


def per_device(points, weights, density, near_pairs, gap_pairs):
    local = packed(points, weights, density)
    near_tables = [from_offset(local, "dev", o, False) for o in near_offsets]
    gap_tables = [from_offset(local, "section", o, True) for o in gap_offsets]
    total, _ = pair_sums("local", near_pairs, local, [])
    near_a, near_b = pair_sums("near", near_pairs, local, near_tables)
    gap_a, gap_b = pair_sums("gap", gap_pairs, local, gap_tables)
    total = total + near_a + gap_a
    for place, offset in enumerate(near_offsets):
        total = total + from_offset(near_b[place], "dev", -offset, False)
    for place, offset in enumerate(gap_offsets):
        total = total + from_offset(gap_b[place], "section", -offset, True)
    return total


def solution(mesh):
    placed = (
        P(None, None, ("section", "dev")),
        P(None, ("section", "dev")),
        P(None, ("section", "dev")),
        P(None, ("section", "dev")),
        P(None, ("section", "dev")),
    )
    return jax.shard_map(
        per_device,
        mesh=mesh,
        in_specs=placed,
        out_specs=P(None, ("section", "dev")),
        check_vma=False,
    )
```

time: 507 us -> 129 us (0.25)
  matrix products: 400 us -> 0 us
  Pallas kernels: 0 us -> 82.1 us
  local copies, waits for them, and re-layouts: 18.1 us -> 3.03 us
  other arithmetic: 15.5 us -> 1.44 us
  between operations: 14.1 us -> 0.23 us
  loops' own time: 12.5 us -> 0 us
  blocking collectives: 12.2 us -> 0 us
  starting transfers between devices: 27.5 us -> 38.2 us
    dot_general x90 -> x0, matrix products: 400 us -> none  [the longest x45 230 us: pair_terms(): jnp.einsum('gab,grb->gra', kernel_tile, load_b, precision=lax.Precision.H...]
    pallas_call x0 -> x4, Pallas kernels: none -> 82.1 us  [the longest x3 80.4 us: pair_sums(): pl.pallas_call(functools.partial(pair_kernel, kind, tables, clusters), ou...]
    scatter-add x4 -> x0, other arithmetic: 13.2 us -> none  [the longest x2 6.63 us: accumulate(): totals = totals.at[:, first_pos].add(terms_a)]
    another operation x1 -> x0, loops' own time: 12.5 us -> none  [accumulate(): terms_a, terms_b = lax.map(one_group, items)]
    all_gather x1 -> x0, blocking collectives: 12.2 us -> none  [facing_part(): facing_table = lax.all_gather(local_table, 'section', axis=1, tiled=True)]
    ppermute x8 -> x14, starting transfers between devices: 27.5 us -> 38.2 us  [from_offset(): return lax.ppermute(block, axis, route)]
    unnamed x16 -> x18, local copies, waits for them, and re-layouts: 8.36 us -> 1.42 us
    gather x10 -> x0, local copies, waits for them, and re-layouts: 5.85 us -> none  [the longest x5 2.93 us: one_group(): block_a = jnp.transpose(blocks[:, first_set], (1, 0, 2))]
  transfers between devices with their start and end apart: 9 -> 14, of which waited for: 1 -> 1; matrix products, arithmetic and copies ran while one was open for 86% -> 1% of each run, Pallas kernels for 0% -> 64%
where the time goes in v1:
time: 129 us; the launch traced here: 127 us
  Pallas kernels  82.1 us (64%)
  starting transfers between devices  38.2 us (30%)
  local copies, waits for them, and re-layouts  3.03 us (2%)
  waiting for transfers between devices  1.64 us (1%)
  other arithmetic  1.44 us (1%)
    pallas_call x3, Pallas kernels, pair_sums(): pl.pallas_call(functools.partial(pair_kernel, kind, tables, clusters), ou...  80.4 us
    ppermute x14, starting transfers between devices, from_offset(): return lax.ppermute(block, axis, route)  38.2 us
  transfers between devices with their start and end apart: 14, of which 1 were waited for; matrix products, arithmetic and copies ran while one was open for 1% of the time, Pallas kernels for 64%

profile of v1, /device:TPU:41, one launch (start us, length us, event | category | flops | bytes accessed | tf_op | source)
XLA Modules:
  0.0 126.6 jit_solution(8038100999160132280)
XLA Ops:
  0.0 1.7 %pack.1.refs_1_ = f32[16,4096]{1,0:T(8,128)} custom-call(f32[3,3,4096]{2,1,0:T(4,128)} %points.1, f32[3,4096]{1,0:T(4,128)} %weights.1, f32[2,4096]{1,0:T(2,128)} %density.1), custom_call_target="tpu_custom_call" | custom-call | tf_op jit(solution)/shard_map/pack/pallas_call | solution.py:301
  1.7 3.1 %collective-permute-start = (f32[16,4096]{1,0:T(8,128)}, f32[16,4096]{1,0:T(8,128)S(1)}, u32[]{:S(2)}, u32[]{:S(2)}) collective-permute-start(f32[16,4096]{1,0:T(8,128)} %pack.1.refs_1_), channel_id=1, source_target_pairs={{0,2},{1,3},{2,4},{3,5},{4,6},{5,7},{6,8},{7,9},{8,10},{9,11},{10,... | collective-permute-start | bytes 786440 | tf_op jit(solution)/shard_map/ppermute | solution.py:316
  4.8 4.0 %collective-permute-start.1 = (f32[16,4096]{1,0:T(8,128)}, f32[16,4096]{1,0:T(8,128)S(1)}, u32[]{:S(2)}, u32[]{:S(2)}) collective-permute-start(f32[16,4096]{1,0:T(8,128)} %pack.1.refs_1_), channel_id=1, source_target_pairs={{0,1},{1,2},{2,3},{3,4},{4,5},{5,6},{6,7},{7,8},{8,9},{9,10},{10,1... | collective-permute-start | bytes 786440 | tf_op jit(solution)/shard_map/ppermute | solution.py:316
  8.8 1.9 %collective-permute-start.2 = (f32[16,4096]{1,0:T(8,128)}, f32[16,4096]{1,0:T(8,128)S(1)}, u32[]{:S(2)}, u32[]{:S(2)}) collective-permute-start(f32[16,4096]{1,0:T(8,128)} %pack.1.refs_1_), channel_id=1, source_target_pairs={{1,0},{2,1},{3,2},{4,3},{5,4},{6,5},{7,6},{8,7},{9,8},{10,9},{11,1... | collective-permute-start | bytes 786440 | tf_op jit(solution)/shard_map/ppermute | solution.py:316
  10.7 4.3 %collective-permute-start.3 = (f32[16,4096]{1,0:T(8,128)}, f32[16,4096]{1,0:T(8,128)S(1)}, u32[]{:S(2)}, u32[]{:S(2)}) collective-permute-start(f32[16,4096]{1,0:T(8,128)} %pack.1.refs_1_), channel_id=1, source_target_pairs={{2,0},{3,1},{4,2},{5,3},{6,4},{7,5},{8,6},{9,7},{10,8},{11,9},{12,... | collective-permute-start | bytes 786440 | tf_op jit(solution)/shard_map/ppermute | solution.py:316
  15.0 0.1 collective-permute-start.4
  15.1 0.0 collective-permute-done.refs_2_
  15.1 0.0 copy-start
  15.1 2.8 %collective-permute-start.5 = (f32[16,4096]{1,0:T(8,128)}, f32[16,4096]{1,0:T(8,128)S(1)}, u32[]{:S(2)}, u32[]{:S(2)}) collective-permute-start(f32[16,4096]{1,0:T(8,128)} %pack.1.refs_1_), channel_id=1, source_target_pairs={{64,0},{96,32},{0,64},{32,96},{65,1},{97,33},{1,65},{33,97},{66,2}... | collective-permute-start | bytes 786440 | tf_op jit(solution)/shard_map/ppermute | solution.py:316
  17.9 0.0 collective-permute-done.1.refs_3_
  17.9 0.0 copy-start.1
  17.9 1.9 %collective-permute-start.6 = (f32[16,4096]{1,0:T(8,128)}, f32[16,4096]{1,0:T(8,128)S(1)}, u32[]{:S(2)}, u32[]{:S(2)}) collective-permute-start(f32[16,4096]{1,0:T(8,128)} %pack.1.refs_1_), channel_id=1, source_target_pairs={{96,0},{0,32},{32,64},{64,96},{97,1},{1,33},{33,65},{65,97},{98,2}... | collective-permute-start | bytes 786440 | tf_op jit(solution)/shard_map/ppermute | solution.py:316
  19.9 0.0 collective-permute-done.2.refs_4_
  19.9 0.0 copy-start.2
  19.9 1.6 %collective-permute-done.3.refs_5_ = f32[16,4096]{1,0:T(8,128)S(1)} collective-permute-done((f32[16,4096]{1,0:T(8,128)}, f32[16,4096]{1,0:T(8,128)S(1)}, u32[]{:S(2)}, u32[]{:S(2)}) %collective-permute-start.3) | collective-permute-done | bytes 262176 | tf_op jit(solution)/shard_map/ppermute | solution.py:316
  21.5 0.0 copy-done
  21.5 0.0 copy-done.1
  21.5 0.0 copy-done.2
  21.5 0.0 copy-start.3
  21.5 0.7 copy-done.3
  22.2 33.3 %pairs_near.1 = (f32[2,4096]{1,0:T(2,128)}, f32[4,2,4096]{2,1,0:T(2,128)}) custom-call(s32[3,128]{1,0:T(4,128)} %refs_0_.4, f32[16,4096]{1,0:T(8,128)} %pack.1.refs_1_, f32[16,4096]{1,0:T(8,128)} %copy-done, f32[16,4096]{1,0:T(8,128)} %copy-done.1, f32[16,4096]{1,0:T(8,128)} %copy-done.2, f32[16,4096]{1,0:T(8,128)} %copy-done.3), custom_call_target="tpu_custom_call" | custom-call | tf_op jit(solution)/shard_map/pairs_near/pallas_call | solution.py:267
  55.5 0.8 slice_bitcast_fusion.6
  56.3 2.0 %collective-permute-start.10 = (f32[2,4096]{1,0:T(2,128)S(1)}, f32[2,4096]{1,0:T(2,128)S(1)}, u32[]{:S(2)}, u32[]{:S(2)}) collective-permute-start(f32[2,4096]{1,0:T(2,128)S(1)} %get-tuple-element.16), channel_id=1, source_target_pairs={{0,2},{1,3},{2,4},{3,5},{4,6},{5,7},{6,8},{7,9},{8,10},{9,11},{10,... | collective-permute-start | bytes 98312 | tf_op jit(solution)/shard_map/ppermute | solution.py:316
  58.3 6.5 %collective-permute-start.7 = (f32[2,4096]{1,0:T(2,128)S(1)}, f32[2,4096]{1,0:T(2,128)S(1)}, u32[]{:S(2)}, u32[]{:S(2)}) collective-permute-start(f32[2,4096]{1,0:T(2,128)S(1)} %get-tuple-element.15), channel_id=1, source_target_pairs={{2,0},{3,1},{4,2},{5,3},{6,4},{7,5},{8,6},{9,7},{10,8},{11,9},{12,... | collective-permute-start | bytes 98312 | tf_op jit(solution)/shard_map/ppermute | solution.py:316
  64.9 0.0 collective-permute-done.4.refs_2_
  64.9 0.0 copy-start.4
  64.9 1.9 %collective-permute-start.8 = (f32[2,4096]{1,0:T(2,128)S(1)}, f32[2,4096]{1,0:T(2,128)S(1)}, u32[]{:S(2)}, u32[]{:S(2)}) collective-permute-start(f32[2,4096]{1,0:T(2,128)S(1)} %get-tuple-element.18), channel_id=1, source_target_pairs={{1,0},{2,1},{3,2},{4,3},{5,4},{6,5},{7,6},{8,7},{9,8},{10,9},{11,1... | collective-permute-start | bytes 98312 | tf_op jit(solution)/shard_map/ppermute | solution.py:316
  66.8 0.0 collective-permute-done.5.refs_3_
  66.9 0.0 copy-start.5
  66.9 3.6 %collective-permute-start.9 = (f32[2,4096]{1,0:T(2,128)S(1)}, f32[2,4096]{1,0:T(2,128)S(1)}, u32[]{:S(2)}, u32[]{:S(2)}) collective-permute-start(f32[2,4096]{1,0:T(2,128)S(1)} %get-tuple-element.17), channel_id=1, source_target_pairs={{0,1},{1,2},{2,3},{3,4},{4,5},{5,6},{6,7},{7,8},{8,9},{9,10},{10,1... | collective-permute-start | bytes 98312 | tf_op jit(solution)/shard_map/ppermute | solution.py:316
  70.5 0.0 collective-permute-done.6.refs_4_
  70.5 0.0 copy-done.4
  70.5 0.0 copy-done.5
  70.5 0.0 copy-start.6
  70.6 0.7 copy-done.6
  71.2 21.9 %pairs_gap.1 = (f32[2,4096]{1,0:T(2,128)}, f32[3,2,4096]{2,1,0:T(2,128)}) custom-call(s32[3,32]{1,0:T(4,128)} %refs_0_.5, f32[16,4096]{1,0:T(8,128)} %pack.1.refs_1_, f32[16,4096]{1,0:T(8,128)} %copy-done.4, f32[16,4096]{1,0:T(8,128)} %copy-done.5, f32[16,4096]{1,0:T(8,128)} %copy-done.6), custom_call_target="tpu_custom_call" | custom-call | tf_op jit(solution)/shard_map/pairs_gap/pallas_call | solution.py:267
  93.1 0.8 slice_bitcast_fusion.2
  93.9 0.1 collective-permute-start.11
  94.0 0.0 collective-permute-done.10
  94.0 3.9 %collective-permute-start.12 = (f32[2,4096]{1,0:T(2,128)S(1)}, f32[2,4096]{1,0:T(2,128)S(1)}, u32[]{:S(2)}, u32[]{:S(2)}) collective-permute-start(f32[2,4096]{1,0:T(2,128)S(1)} %get-tuple-element.21), channel_id=1, source_target_pairs={{64,0},{96,32},{0,64},{32,96},{65,1},{97,33},{1,65},{33,97},{66,2}... | collective-permute-start | bytes 98312 | tf_op jit(solution)/shard_map/ppermute | solution.py:316
  97.9 0.0 collective-permute-done.7
  97.9 0.0 copy-start.7
  97.9 0.0 copy-start.8
  97.9 2.0 %collective-permute-start.13 = (f32[2,4096]{1,0:T(2,128)S(1)}, f32[2,4096]{1,0:T(2,128)S(1)}, u32[]{:S(2)}, u32[]{:S(2)}) collective-permute-start(f32[2,4096]{1,0:T(2,128)S(1)} %get-tuple-element.20), channel_id=1, source_target_pairs={{32,0},{64,32},{96,64},{0,96},{33,1},{65,33},{97,65},{1,97},{34,2}... | collective-permute-start | bytes 98312 | tf_op jit(solution)/shard_map/ppermute | solution.py:316
  99.9 25.3 %pairs_local.1 = (f32[2,4096]{1,0:T(2,128)}, f32[1,8,128]{2,1,0:T(8,128)}) custom-call(s32[3,128]{1,0:T(4,128)} %refs_0_.4, f32[16,4096]{1,0:T(8,128)} %pack.1.refs_1_), custom_call_target="tpu_custom_call" | custom-call | tf_op jit(solution)/shard_map/pairs_local/pallas_call | solution.py:267
  125.1 0.0 collective-permute-done.8
  125.1 0.0 collective-permute-done.9
  125.1 0.0 collective-permute-done.11
  125.2 0.0 collective-permute-done.12
  125.2 0.0 collective-permute-done.13
  125.2 0.0 copy-done.7
  125.2 0.0 copy-done.8
  125.2 1.4 %add_add_fusion = f32[2,4096]{1,0:T(2,128)} fusion(f32[2,4096]{1,0:T(2,128)S(1)} %collective-permute-done.13, f32[2,4096]{1,0:T(2,128)S(1)} %collective-permute-done.12, f32[2,4096]{1,0:T(2,128)S(1)} %collective-permute-done.11, f32[2,4096]{1,0:T(2,128)S(1)} %collective-permute-done.10, f32[2,4096]{1,0:T(2,128)S(1)} %collective-permute-done.9, ...), kind=kLoop, calls=%fused_computation.1 | loop fusion | flops 73728 | bytes 360448 | tf_op jit(solution)/shard_map/add | solution.py:334
Async XLA Ops:
  1.7 13.4 %collective-permute-start = (f32[16,4096]{1,0:T(8,128)}, f32[16,4096]{1,0:T(8,128)S(1)}, u32[]{:S(2)}, u32[]{:S(2)}) collective-permute-start(f32[16,4096]{1,0:T(8,128)} %pack.1.refs_1_), channel_id=1, source_target_pairs={{0,2},{1,3},{2,4},{3,5},{4,6},{5,7},{6,8},{7,9},{8,10},{9,11},{10,... | collective-permute-start | bytes 786440 | tf_op jit(solution)/shard_map/ppermute | solution.py:316
  4.8 13.1 %collective-permute-start.1 = (f32[16,4096]{1,0:T(8,128)}, f32[16,4096]{1,0:T(8,128)S(1)}, u32[]{:S(2)}, u32[]{:S(2)}) collective-permute-start(f32[16,4096]{1,0:T(8,128)} %pack.1.refs_1_), channel_id=1, source_target_pairs={{0,1},{1,2},{2,3},{3,4},{4,5},{5,6},{6,7},{7,8},{8,9},{9,10},{10,1... | collective-permute-start | bytes 786440 | tf_op jit(solution)/shard_map/ppermute | solution.py:316
  8.8 11.1 %collective-permute-start.2 = (f32[16,4096]{1,0:T(8,128)}, f32[16,4096]{1,0:T(8,128)S(1)}, u32[]{:S(2)}, u32[]{:S(2)}) collective-permute-start(f32[16,4096]{1,0:T(8,128)} %pack.1.refs_1_), channel_id=1, source_target_pairs={{1,0},{2,1},{3,2},{4,3},{5,4},{6,5},{7,6},{8,7},{9,8},{10,9},{11,1... | collective-permute-start | bytes 786440 | tf_op jit(solution)/shard_map/ppermute | solution.py:316
  10.7 10.7 %collective-permute-start.3 = (f32[16,4096]{1,0:T(8,128)}, f32[16,4096]{1,0:T(8,128)S(1)}, u32[]{:S(2)}, u32[]{:S(2)}) collective-permute-start(f32[16,4096]{1,0:T(8,128)} %pack.1.refs_1_), channel_id=1, source_target_pairs={{2,0},{3,1},{4,2},{5,3},{6,4},{7,5},{8,6},{9,7},{10,8},{11,9},{12,... | collective-permute-start | bytes 786440 | tf_op jit(solution)/shard_map/ppermute | solution.py:316
  15.0 49.9 %collective-permute-start.4 = (f32[16,4096]{1,0:T(8,128)}, f32[16,4096]{1,0:T(8,128)S(1)}, u32[]{:S(2)}, u32[]{:S(2)}) collective-permute-start(f32[16,4096]{1,0:T(8,128)} %pack.1.refs_1_), channel_id=1, source_target_pairs={{32,0},{64,32},{96,64},{0,96},{33,1},{65,33},{97,65},{1,97},{34,2}... | collective-permute-start | bytes 786440 | tf_op jit(solution)/shard_map/ppermute | solution.py:316
  15.1 6.4 %copy-start = (f32[16,4096]{1,0:T(8,128)}, f32[16,4096]{1,0:T(8,128)S(1)}, u32[]{:S(2)}) copy-start(f32[16,4096]{1,0:T(8,128)S(1)} %collective-permute-done.refs_2_) | copy-start | bytes 786436
  15.1 51.7 %collective-permute-start.5 = (f32[16,4096]{1,0:T(8,128)}, f32[16,4096]{1,0:T(8,128)S(1)}, u32[]{:S(2)}, u32[]{:S(2)}) collective-permute-start(f32[16,4096]{1,0:T(8,128)} %pack.1.refs_1_), channel_id=1, source_target_pairs={{64,0},{96,32},{0,64},{32,96},{65,1},{97,33},{1,65},{33,97},{66,2}... | collective-permute-start | bytes 786440 | tf_op jit(solution)/shard_map/ppermute | solution.py:316
  17.9 3.6 %copy-start.1 = (f32[16,4096]{1,0:T(8,128)}, f32[16,4096]{1,0:T(8,128)S(1)}, u32[]{:S(2)}) copy-start(f32[16,4096]{1,0:T(8,128)S(1)} %collective-permute-done.1.refs_3_) | copy-start | bytes 786436
  17.9 52.6 %collective-permute-start.6 = (f32[16,4096]{1,0:T(8,128)}, f32[16,4096]{1,0:T(8,128)S(1)}, u32[]{:S(2)}, u32[]{:S(2)}) collective-permute-start(f32[16,4096]{1,0:T(8,128)} %pack.1.refs_1_), channel_id=1, source_target_pairs={{96,0},{0,32},{32,64},{64,96},{97,1},{1,33},{33,65},{65,97},{98,2}... | collective-permute-start | bytes 786440 | tf_op jit(solution)/shard_map/ppermute | solution.py:316
  19.9 1.6 %copy-start.2 = (f32[16,4096]{1,0:T(8,128)}, f32[16,4096]{1,0:T(8,128)S(1)}, u32[]{:S(2)}) copy-start(f32[16,4096]{1,0:T(8,128)S(1)} %collective-permute-done.2.refs_4_) | copy-start | bytes 786436
  21.5 0.7 copy-start.3
  56.3 37.7 %collective-permute-start.10 = (f32[2,4096]{1,0:T(2,128)S(1)}, f32[2,4096]{1,0:T(2,128)S(1)}, u32[]{:S(2)}, u32[]{:S(2)}) collective-permute-start(f32[2,4096]{1,0:T(2,128)S(1)} %get-tuple-element.16), channel_id=1, source_target_pairs={{0,2},{1,3},{2,4},{3,5},{4,6},{5,7},{6,8},{7,9},{8,10},{9,11},{10,... | collective-permute-start | bytes 98312 | tf_op jit(solution)/shard_map/ppermute | solution.py:316
  58.3 39.6 %collective-permute-start.7 = (f32[2,4096]{1,0:T(2,128)S(1)}, f32[2,4096]{1,0:T(2,128)S(1)}, u32[]{:S(2)}, u32[]{:S(2)}) collective-permute-start(f32[2,4096]{1,0:T(2,128)S(1)} %get-tuple-element.15), channel_id=1, source_target_pairs={{2,0},{3,1},{4,2},{5,3},{6,4},{7,5},{8,6},{9,7},{10,8},{11,9},{12,... | collective-permute-start | bytes 98312 | tf_op jit(solution)/shard_map/ppermute | solution.py:316
  64.9 5.6 %copy-start.4 = (f32[16,4096]{1,0:T(8,128)}, f32[16,4096]{1,0:T(8,128)S(1)}, u32[]{:S(2)}) copy-start(f32[16,4096]{1,0:T(8,128)S(1)} %collective-permute-done.4.refs_2_) | copy-start | bytes 786436
  64.9 60.2 %collective-permute-start.8 = (f32[2,4096]{1,0:T(2,128)S(1)}, f32[2,4096]{1,0:T(2,128)S(1)}, u32[]{:S(2)}, u32[]{:S(2)}) collective-permute-start(f32[2,4096]{1,0:T(2,128)S(1)} %get-tuple-element.18), channel_id=1, source_target_pairs={{1,0},{2,1},{3,2},{4,3},{5,4},{6,5},{7,6},{8,7},{9,8},{10,9},{11,1... | collective-permute-start | bytes 98312 | tf_op jit(solution)/shard_map/ppermute | solution.py:316
  66.9 3.7 %copy-start.5 = (f32[16,4096]{1,0:T(8,128)}, f32[16,4096]{1,0:T(8,128)S(1)}, u32[]{:S(2)}) copy-start(f32[16,4096]{1,0:T(8,128)S(1)} %collective-permute-done.5.refs_3_) | copy-start | bytes 786436
  66.9 58.3 %collective-permute-start.9 = (f32[2,4096]{1,0:T(2,128)S(1)}, f32[2,4096]{1,0:T(2,128)S(1)}, u32[]{:S(2)}, u32[]{:S(2)}) collective-permute-start(f32[2,4096]{1,0:T(2,128)S(1)} %get-tuple-element.17), channel_id=1, source_target_pairs={{0,1},{1,2},{2,3},{3,4},{4,5},{5,6},{6,7},{7,8},{8,9},{9,10},{10,1... | collective-permute-start | bytes 98312 | tf_op jit(solution)/shard_map/ppermute | solution.py:316
  70.5 0.7 copy-start.6
  93.9 31.2 %collective-permute-start.11 = (f32[2,4096]{1,0:T(2,128)S(1)}, f32[2,4096]{1,0:T(2,128)S(1)}, u32[]{:S(2)}, u32[]{:S(2)}) collective-permute-start(f32[2,4096]{1,0:T(2,128)S(1)} %get-tuple-element.19), channel_id=1, source_target_pairs={{96,0},{0,32},{32,64},{64,96},{97,1},{1,33},{33,65},{65,97},{98,2}... | collective-permute-start | bytes 98312 | tf_op jit(solution)/shard_map/ppermute | solution.py:316
  94.0 31.2 %collective-permute-start.12 = (f32[2,4096]{1,0:T(2,128)S(1)}, f32[2,4096]{1,0:T(2,128)S(1)}, u32[]{:S(2)}, u32[]{:S(2)}) collective-permute-start(f32[2,4096]{1,0:T(2,128)S(1)} %get-tuple-element.21), channel_id=1, source_target_pairs={{64,0},{96,32},{0,64},{32,96},{65,1},{97,33},{1,65},{33,97},{66,2}... | collective-permute-start | bytes 98312 | tf_op jit(solution)/shard_map/ppermute | solution.py:316
  97.9 27.3 %copy-start.7 = (f32[2,4096]{1,0:T(2,128)S(1)}, f32[2,4096]{1,0:T(2,128)}, u32[]{:S(2)}) copy-start(f32[2,4096]{1,0:T(2,128)} %get-tuple-element.11) | copy-start | bytes 98308
  97.9 27.3 %copy-start.8 = (f32[2,4096]{1,0:T(2,128)S(1)}, f32[2,4096]{1,0:T(2,128)}, u32[]{:S(2)}) copy-start(f32[2,4096]{1,0:T(2,128)} %get-tuple-element.12) | copy-start | bytes 98308
  97.9 27.3 %collective-permute-start.13 = (f32[2,4096]{1,0:T(2,128)S(1)}, f32[2,4096]{1,0:T(2,128)S(1)}, u32[]{:S(2)}, u32[]{:S(2)}) collective-permute-start(f32[2,4096]{1,0:T(2,128)S(1)} %get-tuple-element.20), channel_id=1, source_target_pairs={{32,0},{64,32},{96,64},{0,96},{33,1},{65,33},{97,65},{1,97},{34,2}... | collective-permute-start | bytes 98312 | tf_op jit(solution)/shard_map/ppermute | solution.py:316
